TPU v7x, 256 devices: a whole 4x4x8 slice. The times are simulated.
256 devices in a mesh: branch: 2 (over core), seq: 64 (over x_hi, y, z), blk: 2 (over x_lo).
Axes of the slice: x: 4 (x_hi: 2, x_lo: 2; x = x_hi * 2 + x_lo), y: 4, z: 8, core: 2. Of those that a mesh axis runs over, the one named last changes fastest.
Arguments:
- query: bfloat16 [2, 4608, 3072], P('branch', ('seq', 'blk')), may hold values from -10 to 10
- key: bfloat16 [2, 4608, 3072], P('branch', ('seq', 'blk')), may hold values from -10 to 10
- value: bfloat16 [2, 4608, 3072], P('branch', ('seq', 'blk')), may hold values from -6 to 6
- out_weight: bfloat16 [3072, 3072], P('blk'), may hold values from -0.109375 to 0.109375
Outputs:
- guided: bfloat16 [4608, 3072], P(('seq', 'blk'), 'branch')
All inputs are finite; a program needn't handle non-finite values.
Results may differ from a plain program's by a relative error of at most 0.015.
Values may be sent and summed in bfloat16 or wider, within the bound.
A program may use at most 256 MiB of HBM per device.

v0:
```python
import jax
import jax.numpy as jnp
from jax import lax
from jax.sharding import PartitionSpec as P

HD = 128
GRIDW = 256


guidance = 4.0


def from_partner(value, axis, apart):
    mask = 2**apart
    pairs = [(source, source ^ mask) for source in range(lax.axis_size(axis))]
    return lax.ppermute(value, axis, pairs)


def pair_angles(positions):
    time_dim = HD // 8
    side_dim = (HD - time_dim) // 2
    index = jnp.arange(side_dim // 2).astype(jnp.float32)
    freq = jnp.power(jnp.float32(10000.0), -2.0 * index / side_dim)
    row_at = (positions // GRIDW).astype(jnp.float32)
    col_at = (positions % GRIDW).astype(jnp.float32)
    still = jnp.zeros((positions.shape[0], time_dim // 2), jnp.float32)
    return jnp.concatenate(
        [still, row_at[:, None] * freq[None, :], col_at[:, None] * freq[None, :]], axis=1
    )


def rotate(values, positions):
    count = values.shape[0]
    pairs = values.astype(jnp.float32).reshape(count, -1, HD // 2, 2)
    angle = pair_angles(positions)[:, None, :]
    cosine = jnp.cos(angle)
    sine = jnp.sin(angle)
    first = pairs[..., 0] * cosine - pairs[..., 1] * sine
    second = pairs[..., 0] * sine + pairs[..., 1] * cosine
    return jnp.stack([first, second], axis=-1).reshape(count, -1).astype(jnp.bfloat16)


def start_state(queries):
    heads = queries.shape[1] // HD
    count = queries.shape[0]
    return (
        jnp.full((heads, count), -1e30, jnp.float32),
        jnp.zeros((heads, count), jnp.float32),
        jnp.zeros((heads, count, HD), jnp.float32),
    )


def make_step(queries, state, piece):
    heads = queries.shape[1] // HD
    q_heads = queries.reshape(queries.shape[0], heads, HD)
    top, total, acc = state
    k_piece, v_piece = piece
    k_heads = k_piece.reshape(k_piece.shape[0], heads, HD)
    v_heads = v_piece.reshape(v_piece.shape[0], heads, HD)
    scores = jnp.einsum(
        "qhd,khd->hqk", q_heads, k_heads, preferred_element_type=jnp.float32
    ) * HD ** (-0.5)
    new_top = jnp.maximum(top, jnp.max(scores, axis=-1))
    expo = jnp.exp(scores - new_top[..., None])
    total = jnp.sum(expo, axis=-1)
    acc = jnp.einsum(
        "hqk,khd->hqd", expo.astype(jnp.bfloat16), v_heads, preferred_element_type=jnp.float32
    )
    return (new_top, total, acc)


def finish(state):
    top, total, acc = state
    mixed = acc / total[..., None]
    return mixed.transpose(1, 0, 2).reshape(acc.shape[1], acc.shape[0] * HD).astype(jnp.bfloat16)


def shards(query, key, value, out_weight):
    rows = query.shape[1]
    place = lax.axis_index("seq") * lax.axis_size("blk") + lax.axis_index("blk")
    positions = place * rows + jnp.arange(rows, dtype=jnp.int32)
    turned_q = rotate(query[0], positions)
    turned_k = rotate(key[0], positions)
    values_own = value[0]
    local_q, local_k, local_v = (
        lax.all_to_all(turned_q, "blk", split_axis=1, concat_axis=0, tiled=True),
        lax.all_to_all(turned_k, "blk", split_axis=1, concat_axis=0, tiled=True),
        lax.all_to_all(values_own, "blk", split_axis=1, concat_axis=0, tiled=True),
    )
    state = make_step(
        local_q,
        start_state(local_q),
        (
            lax.all_gather(local_k, "seq", axis=0, tiled=True),
            lax.all_gather(local_v, "seq", axis=0, tiled=True),
        ),
    )
    split_out = finish(state)
    term = jnp.dot(split_out, out_weight, preferred_element_type=jnp.float32)
    projected = lax.psum_scatter(
        lax.optimization_barrier(term.astype(jnp.bfloat16))
        .astype(jnp.float32)
        .astype(jnp.bfloat16),
        "blk",
        scatter_dimension=0,
        tiled=True,
    )
    half_width = projected.shape[1] // 2
    branch_at = lax.axis_index("branch")
    outgoing = lax.dynamic_slice_in_dim(projected, (1 - branch_at) * half_width, half_width, 1)
    own_cols = lax.dynamic_slice_in_dim(projected, branch_at * half_width, half_width, 1)
    partner = from_partner(outgoing, "branch", 0)
    first_branch = branch_at == 0
    cond = jnp.where(first_branch, own_cols, partner).astype(jnp.float32)
    uncond = jnp.where(first_branch, partner, own_cols).astype(jnp.float32)
    return (uncond + guidance * (cond - uncond)).astype(jnp.bfloat16)


def solution(mesh):
    in_specs = (
        P("branch", ("seq", "blk"), None),
        P("branch", ("seq", "blk"), None),
        P("branch", ("seq", "blk"), None),
        P("blk", None),
    )
    out_specs = P(("seq", "blk"), "branch")
    return jax.shard_map(shards, mesh=mesh, in_specs=in_specs, out_specs=out_specs, check_vma=False)
```

profile of v0, /device:TPU:1, one launch (start us, length us, event | category | flops | bytes accessed | tf_op | source)
XLA Modules:
  0.0 494.4 jit_solution(1154415217662198789)
XLA Ops:
  6.5 0.0 copy-start
  6.5 0.0 all-gather.3.cloned.1.call-start
  6.6 1.3 copy.16
  7.9 1.3 copy.18
  9.2 0.1 broadcast_multiply_fusion.1
  9.3 0.2 fusion.25
  9.5 4.9 subtract_convert_fusion.1
  14.4 2.1 pad_maximum_fusion.1
  16.5 0.3 copy.19
  16.8 7.0 %all_to_all.48 = bf16[36,2,1536]{2,0,1:T(8,128)(2,1)S(1)} all-to-all(bf16[36,2,1536]{2,0,1:T(8,128)(2,1)S(1)} %copy.19), channel_id=1, replica_groups=mesh['branch'=2,'seq'=64,'blk'=2] {'blk'}, dimensions={1} | all-to-all | bytes 442368 | tf_op jit(solution)/shard_map/all_to_all | solution.py:87
  23.8 0.7 all_to_all.40
  24.6 0.0 all-gather.3.cloned.1.call-update
  24.6 0.0 all-gather.5.cloned.1.call-start
  24.6 0.0 copy-done
  24.7 0.1 all_to_all.41
  24.8 6.3 %all_to_all.49 = bf16[36,2,1536]{2,0,1:T(8,128)(2,1)S(1)} all-to-all(bf16[36,2,1536]{2,0,1:T(8,128)(2,1)S(1)} %copy.23), channel_id=1, replica_groups=mesh['branch'=2,'seq'=64,'blk'=2] {'blk'}, dimensions={1} | all-to-all | bytes 442368 | tf_op jit(solution)/shard_map/all_to_all | solution.py:88
  31.1 0.7 all_to_all.44
  31.9 0.0 all-gather.5.cloned.1.call-update
  31.9 0.0 all-reduce.3.cloned.1.call-start
  31.9 3.4 pad_maximum_fusion
  35.4 0.3 copy.17
  35.7 6.3 %all_to_all.50 = bf16[36,2,1536]{2,0,1:T(8,128)(2,1)S(1)} all-to-all(bf16[36,2,1536]{2,0,1:T(8,128)(2,1)S(1)} %copy.17), channel_id=1, replica_groups=mesh['branch'=2,'seq'=64,'blk'=2] {'blk'}, dimensions={1} | all-to-all | bytes 442368 | tf_op jit(solution)/shard_map/all_to_all | solution.py:86
  42.0 0.2 reshape.144
  42.2 177.0 %all-gather.3.cloned.1.call-done = bf16[4608,1536]{1,0:T(8,128)(2,1)} async-done(((bf16[72,1536]{1,0:T(8,128)(2,1)}), bf16[4608,1536]{1,0:T(8,128)(2,1)}) %all-gather.3.cloned.1.call-update) | async-done | bytes 14155792 | tf_op jit(solution)/shard_map/all_gather | solution.py:94
  219.2 18.7 %copy.20 = bf16[4608,1536]{0,1:T(8,128)(2,1)} copy(bf16[4608,1536]{1,0:T(8,128)(2,1)} %all-gather.3.cloned.1.call-done) | data formatting | bytes 28311552 | tf_op jit(solution)/shard_map/all_gather | solution.py:94
  237.9 13.1 %multiply_reduce_fusion = (f32[12,72]{1,0:T(8,128)S(1)}, f32[12,72,4608]{2,1,0:T(8,128)}) fusion(bf16[4608,12,128]{0,2,1:T(8,128)(2,1)} %bitcast.28, bf16[72,12,128]{2,1,0:T(8,128)(2,1)S(1)} %reshape.144), kind=kOutput, calls=%fused_computation.1 | convolution fusion | flops 1027177600 | bytes 30305664 | tf_op jit(solution)/shard_map/qhd,khd->hqk/dot_general | solution.py:60
  251.0 8.3 %fusion = f32[12,72]{1,0:T(8,128)S(1)} fusion(f32[12,72,4608]{2,1,0:T(8,128)} %get-tuple-element.16, f32[12,72]{1,0:T(8,128)S(1)} %broadcast_maximum_fusion), kind=kLoop, calls=%fused_computation.2 | loop fusion | flops 11943072 | bytes 15932160 | tf_op jit(solution)/shard_map/reduce_sum | solution.py:65
  259.3 150.8 %all-gather.5.cloned.1.call-done = bf16[4608,1536]{1,0:T(8,128)(2,1)} async-done(((bf16[72,1536]{1,0:T(8,128)(2,1)}), bf16[4608,1536]{1,0:T(8,128)(2,1)}) %all-gather.5.cloned.1.call-update) | async-done | bytes 14155792 | tf_op jit(solution)/shard_map/all_gather | solution.py:95
  410.2 18.7 %copy.24 = bf16[4608,1536]{0,1:T(8,128)(2,1)} copy(bf16[4608,1536]{1,0:T(8,128)(2,1)} %all-gather.5.cloned.1.call-done) | data formatting | bytes 28311552 | tf_op jit(solution)/shard_map/all_gather | solution.py:95
  428.9 12.4 %fusion.15 = bf16[12,9,8,128]{3,2,1,0:T(8,128)(2,1)S(1)} fusion(bf16[4608,12,128]{0,2,1:T(8,128)(2,1)} %bitcast.27, f32[12,72,4608]{2,1,0:T(8,128)} %get-tuple-element.16, f32[12,72]{1,0:T(8,128)S(1)} %broadcast_maximum_fusion, f32[72,12]{0,1:T(8,128)S(1)} %bitcast.36), kind=kOutput, calls=%fused_computation.11 | convolution fusion | flops 1031380992 | bytes 30309120 | tf_op jit(solution)/shard_map/hqk,khd->hqd/dot_general | solution.py:66
  441.2 0.0 copy-start.1
  441.2 6.2 %convolution_convert_fusion = bf16[72,3072]{1,0:T(8,128)(2,1)} fusion(bf16[1536,3072]{1,0:T(8,128)(2,1)} %param.7, bf16[12,9,8,128]{3,2,1,0:T(8,128)(2,1)S(1)} %fusion.15), kind=kOutput, calls=%fused_computation.7 | convolution fusion | flops 679698432 | bytes 10100736 | tf_op jit(solution)/shard_map/dot_general | solution.py:99
  447.5 0.0 all-reduce.3.cloned.1.call-update
  447.5 0.0 copy-done.1
  447.5 0.6 dynamic-slice
  448.8 34.6 %all-reduce.3.cloned.1.call-done = bf16[72,3072]{1,0:T(8,128)(2,1)} async-done(((bf16[72,3072]{1,0:T(8,128)(2,1)}), bf16[72,3072]{1,0:T(8,128)(2,1)}) %all-reduce.3.cloned.1.call-update) | async-done | bytes 442384
  483.4 1.0 dynamic_slice.6
  484.4 0.8 collective-permute-start
  485.2 1.0 collective-permute-done
  486.2 1.7 fusion.19
  (6 shorter events, 0.1 us)
Async XLA Ops:
  6.5 18.1 %copy-start = (bf16[1,36,3072]{2,1,0:T(8,128)(2,1)S(1)}, bf16[1,36,3072]{2,1,0:T(8,128)(2,1)}, u32[]{:S(2)}) copy-start(bf16[1,36,3072]{2,1,0:T(8,128)(2,1)} %param.6) | copy-start | bytes 663556
  6.5 212.7 %all-gather.3.cloned.1.call-start = ((), (), s32[]{:S(2)}) async-start(), calls=%async_computation.3 | async-start | bytes 14376960 | tf_op jit(solution)/shard_map/all_gather | solution.py:94
  24.6 385.6 %all-gather.5.cloned.1.call-start = ((), (), s32[]{:S(2)}) async-start(), calls=%async_computation.4 | async-start | bytes 14376960 | tf_op jit(solution)/shard_map/all_gather | solution.py:95
  31.9 451.5 %all-reduce.3.cloned.1.call-start = ((), (), s32[]{:S(2)}) async-start(), calls=%async_computation.5 | async-start | bytes 884736
  441.2 6.3 %copy-start.1 = (u32[256]{0:T(256)S(1)}, u32[256]{0:T(256)}, u32[]{:S(2)}) copy-start(u32[256]{0:T(256)} %constant.78) | copy-start | bytes 3076
  484.4 1.7 collective-permute-start
Sparse Core Ops, SparseCore 0:
  24.7 194.4 all-gather.2
  222.9 187.1 all-gather.4
  447.6 35.7 all-reduce.2
where the time goes:
time: 496 us; the launch traced here: 494 us
  waiting for transfers between devices  364 us (73%)
  local copies, waits for them, and re-layouts  44.1 us (9%)
  matrix products  31.7 us (6%)
  other arithmetic  20.7 us (4%)
  blocking collectives  19.7 us (4%)
  between operations  13.9 us (3%)
    all_gather x1, waiting for transfers between devices, shards(): lax.all_gather(local_k, 'seq', axis=0, tiled=True)  177 us
    all_gather x1, waiting for transfers between devices, shards(): lax.all_gather(local_v, 'seq', axis=0, tiled=True)  151 us
    unnamed x4, waiting for transfers between devices  34.7 us
    all_gather x1, local copies, waits for them, and re-layouts, shards(): lax.all_gather(local_k, 'seq', axis=0, tiled=True)  18.7 us
    all_gather x1, local copies, waits for them, and re-layouts, shards(): lax.all_gather(local_v, 'seq', axis=0, tiled=True)  18.7 us
    dot_general x1, matrix products, make_step(): jnp.einsum('qhd,khd->hqk', q_heads, k_heads, preferred_element_type=jnp.f...  13.1 us
    dot_general x1, matrix products, make_step(): jnp.einsum('hqk,khd->hqd', expo.astype(jnp.bfloat16), v_heads, preferred_...  12.4 us
  transfers between devices with their start and end apart: 4, of which 4 were waited for; matrix products, arithmetic and copies ran while one was open for 9% of the time, Pallas kernels for 0%

commit v1 on v0

v1 whole, which is shorter than its diff:
```python
import functools

import jax
import jax.numpy as jnp
import numpy as np
from jax import lax
from jax.experimental import pallas as pl
from jax.experimental.pallas import tpu as pltpu
from jax.sharding import PartitionSpec as P

HD = 128
GRIDW = 256
GUIDANCE = 4.0
F32 = jnp.float32
BF16 = jnp.bfloat16
MESH = pl.DeviceIdType.MESH

NJ = 3
NZ = 8
NY = 4
ROWS = 36
MAIN = 32
REM = ROWS - MAIN
TOK = NZ * ROWS
QS = 4 * TOK
KS = NY * TOK
QT = 384
WIN = 384
SCALE = float(HD**-0.5 / np.log(2.0))


def tables(places):
    time_dim = HD // 8
    side_dim = (HD - time_dim) // 2
    index = np.arange(side_dim // 2).astype(np.float32)
    freq = np.power(np.float32(10000.0), -2.0 * index / side_dim).astype(np.float32)
    at = np.arange(places * ROWS)
    row = (at // GRIDW).astype(np.float32)[:, None] * freq[None, :]
    col = (at % GRIDW).astype(np.float32)[:, None] * freq[None, :]
    still = np.zeros((places * ROWS, time_dim // 2), np.float32)
    angle = np.repeat(np.concatenate([still, row, col], axis=1), 2, axis=1).astype(np.float64)
    sign = np.where(np.arange(HD) % 2 == 0, -1.0, 1.0)
    both = np.stack([np.cos(angle), np.sin(angle) * sign]).astype(np.float32)
    out = np.zeros((places, 2, 40, HD), np.float32)
    out[:, :, :ROWS] = both.reshape(2, places, ROWS, HD).transpose(1, 0, 2, 3)
    return out


def turn(x, cos, sin):
    even = lax.broadcasted_iota(jnp.int32, x.shape, 1) % 2 == 0
    swapped = jnp.where(even, pltpu.roll(x, HD - 1, 1), pltpu.roll(x, 1, 1))
    return x * cos + swapped * sin


def pick(shape, source):
    row = lax.broadcasted_iota(jnp.int32, shape, 0)
    col = lax.broadcasted_iota(jnp.int32, shape, 1)
    return jnp.where(col == source(row), 1.0, 0.0).astype(BF16)


def dot(a, b):
    return jnp.dot(a, b, preferred_element_type=F32)


def kernel(
    q_ref, k_ref, v_ref, w_ref, tab_ref, o_ref,
    tab, rtab, send_a, recv_a, qall, kv, vt, obuf, stat, mo, mst, wt, cbuf, recv_c, sib_c, gbuf,
    acc, dsend, drecv, wv,
    tab_sem, w_sem, a_send, a_recv, q_send, q_recv, kv_send, kv_recv, f_send, f_recv,
    m_send, m_recv, n_send, n_recv, c_send, c_recv, s_send, s_recv, d_send, d_recv,
):
    c = lax.axis_index("branch")
    s = lax.axis_index("seq")
    xl = lax.axis_index("blk")
    xh = s // 32
    y = (s // 8) % 4
    z = s % 8
    place = s * 2 + xl
    slot = c * 2 + xl

    tab_copy = pltpu.make_async_copy(tab_ref.at[place], tab, tab_sem)
    tab_copy.start()
    w_copies = []
    for j in range(NJ):
        for t in range(4):
            w_copies.append(
                pltpu.make_async_copy(
                    w_ref.at[pl.ds((t * NJ + j) * HD, HD), pl.ds(pl.multiple_of(c * 1536, 1536), 1536)],
                    wv.at[j, pl.ds(t * HD, HD)],
                    w_sem.at[j, t],
                )
            )
            w_copies[-1].start()

    def far(zz, blk):
        return (xh, (c * 4 + y) * 8 + zz, blk)

    def ring(step):
        return (c, (xh * 4 + (y + step) % 4) * 8 + z, xl)

    def near(step):
        other = (slot + step) % 4
        return (other // 2, s, other % 2), other

    barrier = pltpu.get_barrier_semaphore()

    @pl.loop(0, NZ)
    def _(zz):
        for blk in range(2):
            @pl.when(jnp.logical_not((xh == c) & (zz == z) & (xl == blk)))
            def _():
                pl.semaphore_signal(barrier, inc=1, device_id=far(zz, blk), device_id_type=MESH)

    for step in range(1, 4):
        pl.semaphore_signal(barrier, inc=1, device_id=ring(step), device_id_type=MESH)
        pl.semaphore_signal(barrier, inc=1, device_id=near(step)[0], device_id_type=MESH)

    def own(zz):
        return (xh == c) & (zz == z)

    def a_copy(j, zz):
        return pltpu.make_async_remote_copy(
            src_ref=send_a.at[j, zz], dst_ref=recv_a.at[j, z],
            send_sem=a_send.at[j, zz], recv_sem=a_recv.at[j, z],
            device_id=far(zz, xl), device_id_type=MESH,
        )

    def a_local(j):
        return pltpu.make_async_copy(send_a.at[j, z], recv_a.at[j, z], a_recv.at[j, z])

    def a_arrival(j, zz):
        return pltpu.make_async_remote_copy(
            src_ref=send_a.at[j, zz], dst_ref=recv_a.at[j, zz],
            send_sem=a_send.at[j, zz], recv_sem=a_recv.at[j, zz],
            device_id=far(zz, xl), device_id_type=MESH,
        )

    tab_copy.wait()
    rtab[0, 0:4] = tab[0, 32:36] * SCALE
    rtab[0, 4:8] = tab[0, 32:36]
    rtab[1, 0:4] = tab[1, 32:36] * SCALE
    rtab[1, 4:8] = tab[1, 32:36]

    def prepare(j):
        @pl.loop(0, NZ)
        def _(zz):
            cols = pl.ds(pl.multiple_of((zz * NJ + j) * HD, HD), HD)
            cos, sin = tab[0, 0:MAIN], tab[1, 0:MAIN]
            q = turn(q_ref[0, 0:MAIN, cols].astype(F32), cos * SCALE, sin * SCALE)
            k = turn(k_ref[0, 0:MAIN, cols].astype(F32), cos, sin)
            send_a[j, zz, 0:32] = q.astype(BF16)
            send_a[j, zz, 32:64] = k.astype(BF16)
            send_a[j, zz, 64:96] = v_ref[0, 0:MAIN, cols]
            qk = jnp.concatenate(
                [q_ref[0, MAIN:ROWS, cols].astype(F32), k_ref[0, MAIN:ROWS, cols].astype(F32)], axis=0
            )
            v4 = v_ref[0, MAIN:ROWS, cols].astype(F32)
            rest = jnp.concatenate([turn(qk, rtab[0], rtab[1]), v4, jnp.zeros_like(v4)], axis=0)
            send_a[j, zz, 96:112] = rest.astype(BF16)

    def depart(j):
        @pl.loop(1, NZ + 1)
        def _(i):
            zz = (z + i) % NZ

            @pl.when(own(zz))
            def _():
                a_local(j).start()

            @pl.when(jnp.logical_not(own(zz)))
            def _():
                a_copy(j, zz).start()

    prepare(0)
    pl.semaphore_wait(barrier, jnp.where(xh == c, 21, 22))
    depart(0)
    for j in range(1, NJ):
        prepare(j)
        depart(j)

    def q_copy(j, step):
        device, other = near(step)
        return pltpu.make_async_remote_copy(
            src_ref=qall.at[j, slot], dst_ref=qall.at[j, slot],
            send_sem=q_send.at[j, step - 1], recv_sem=q_recv.at[j, 3 - step],
            device_id=device, device_id_type=MESH,
        )

    def q_arrival(j, step):
        device, other = near(step)
        return pltpu.make_async_remote_copy(
            src_ref=qall.at[j, slot], dst_ref=qall.at[j, other],
            send_sem=q_send.at[j, step - 1], recv_sem=q_recv.at[j, step - 1],
            device_id=device, device_id_type=MESH,
        )

    def kv_copy(j, way):
        return pltpu.make_async_remote_copy(
            src_ref=kv.at[j, 0], dst_ref=kv.at[j, 1 + way],
            send_sem=kv_send.at[j, way], recv_sem=kv_recv.at[j, way],
            device_id=ring(1 if way == 0 else 3), device_id_type=MESH,
        )

    def f_copy(j, way):
        return pltpu.make_async_remote_copy(
            src_ref=kv.at[j, 1 + way, way], dst_ref=kv.at[j, 3, way],
            send_sem=f_send.at[j, way], recv_sem=f_recv.at[j, way],
            device_id=ring(1 if way == 0 else 3), device_id_type=MESH,
        )

    def gather(j):
        for zz in range(NZ):
            a_arrival(j, zz).wait_recv()
        for zz in range(NZ):
            kv[j, 0, 0, zz * 32 : zz * 32 + 32] = recv_a[j, zz, 32:64]
            kv[j, 0, 1, zz * 32 : zz * 32 + 32] = recv_a[j, zz, 64:96]
            qall[j, slot, zz * 32 : zz * 32 + 32] = recv_a[j, zz, 0:32]
        rest = recv_a[j, :, 96:112, :].reshape(NZ * 16, HD)
        order = pick((96, 128), lambda r: (r % 32) // 4 * 16 + r // 32 * 4 + r % 4)
        rest = dot(order, rest).astype(BF16)
        kv[j, 0, 0, 256:288] = rest[32:64]
        kv[j, 0, 1, 256:288] = rest[64:96]
        qall[j, slot, 256:288] = rest[0:32]
        for way in range(2):
            kv_copy(j, way).start()
        for step in range(1, 4):
            q_copy(j, step).start()

    def forward(j):
        for way in range(2):
            kv_copy(j, way).wait_recv()
            f_copy(j, way).start()

    def m_copies(j, step):
        device, other = near(step)
        return (
            pltpu.make_async_remote_copy(
                src_ref=obuf.at[j, pl.ds(pl.multiple_of(other * TOK, 32), TOK)], dst_ref=mo.at[j, slot],
                send_sem=m_send.at[j, step - 1], recv_sem=m_recv.at[j, 3 - step],
                device_id=device, device_id_type=MESH,
            ),
            pltpu.make_async_remote_copy(
                src_ref=stat.at[j, :, pl.ds(pl.multiple_of(other * 256, 256), WIN)], dst_ref=mst.at[j, slot],
                send_sem=n_send.at[j, step - 1], recv_sem=n_recv.at[j, 3 - step],
                device_id=device, device_id_type=MESH,
            ),
        )

    def m_arrivals(j, step):
        device, other = near(step)
        return (
            pltpu.make_async_remote_copy(
                src_ref=mo.at[j, slot], dst_ref=mo.at[j, other],
                send_sem=m_send.at[j, step - 1], recv_sem=m_recv.at[j, step - 1],
                device_id=device, device_id_type=MESH,
            ),
            pltpu.make_async_remote_copy(
                src_ref=mst.at[j, slot], dst_ref=mst.at[j, other],
                send_sem=n_send.at[j, step - 1], recv_sem=n_recv.at[j, step - 1],
                device_id=device, device_id_type=MESH,
            ),
        )

    def attend(j):
        for step in range(1, 4):
            q_arrival(j, step).wait_recv()
        for way in range(2):
            f_copy(j, way).wait_recv()
        for t in range(NY):
            vt[:, t * TOK : (t + 1) * TOK] = kv[j, t, 1].astype(F32).T.astype(BF16)
        stat[j] = jnp.zeros((8, QS), F32)
        queries = qall.at[j].reshape(QS, HD)

        @pl.loop(0, QS // QT)
        def _(t):
            rows = pl.ds(pl.multiple_of(t * QT, QT), QT)
            q = queries[rows, :]
            keys = kv[j, :, 0].reshape(KS, HD)
            scores = lax.dot_general(keys, q, (((1,), (1,)), ((), ())), preferred_element_type=F32)
            top = jnp.max(scores, axis=0, keepdims=True)
            expo = jnp.exp2(scores - top)
            total = jnp.sum(expo, axis=0, keepdims=True)
            mixed = dot(vt[...], expo.astype(BF16)) / total
            stat[j, 0:1, rows] = top
            stat[j, 1:2, rows] = total
            obuf[j, rows, :] = mixed.T.astype(BF16)

        for step in range(1, 4):
            for copy in m_copies(j, step):
                copy.start()
        mo[j, slot] = obuf[j, pl.ds(pl.multiple_of(slot * TOK, 32), TOK), :]
        mst[j, slot] = stat[j, :, pl.ds(pl.multiple_of(slot * 256, 256), WIN)]

    def c_copy(j, zz):
        return pltpu.make_async_remote_copy(
            src_ref=cbuf.at[j, zz], dst_ref=recv_c.at[j, xl, z % 4],
            send_sem=c_send.at[j, zz], recv_sem=c_recv.at[j, xl, z % 4],
            device_id=far(zz, z // 4), device_id_type=MESH,
        )

    def c_own(zz):
        return (xh == c) & (zz == z) & (z // 4 == xl)

    def merge(j):
        for step in range(1, 4):
            for copy in m_arrivals(j, step):
                copy.wait_recv()
        tops = [mst[j, i, 0:1, :] for i in range(4)]
        top = jnp.maximum(jnp.maximum(tops[0], tops[1]), jnp.maximum(tops[2], tops[3]))
        parts = [mst[j, i, 1:2, :] * jnp.exp2(tops[i] - top) for i in range(4)]
        total = (parts[0] + parts[1]) + (parts[2] + parts[3])
        share = jnp.concatenate([p / total for p in parts] + [jnp.zeros((124, WIN), F32)], axis=0)
        wt[...] = share.T
        share = wt[pl.ds(pl.multiple_of(slot * 32, 32), TOK), :]
        mixed = share[:, 0:1] * mo[j, 0].astype(F32)
        for i in range(1, 4):
            mixed += share[:, i : i + 1] * mo[j, i].astype(F32)
        mixed = mixed.astype(BF16)
        order = pick((128, 32), lambda r: jnp.where(r % 16 < 4, r // 16 * 4 + r % 16, -1))
        rest = dot(order, mixed[256:288]).astype(BF16)
        for zz in range(NZ):
            cbuf[j, zz, 0:32] = mixed[zz * 32 : zz * 32 + 32]
            cbuf[j, zz, 32:48] = rest[zz * 16 : zz * 16 + 16]

        @pl.loop(1, NZ + 1)
        def _(i):
            zz = (z + i) % NZ

            @pl.when(c_own(zz))
            def _():
                pltpu.make_async_copy(cbuf.at[j, z], recv_c.at[j, xl, z % 4], c_recv.at[j, xl, z % 4]).start()

            @pl.when(jnp.logical_not(c_own(zz)))
            def _():
                c_copy(j, zz).start()

    sibling = (1 - c, s, xl)

    def s_copy(j):
        return pltpu.make_async_remote_copy(
            src_ref=recv_c.at[j], dst_ref=sib_c.at[j],
            send_sem=s_send.at[j], recv_sem=s_recv.at[j],
            device_id=sibling, device_id_type=MESH,
        )

    def share_out(j):
        for blk in range(2):
            for t in range(4):
                pltpu.make_async_remote_copy(
                    src_ref=cbuf.at[j, 0], dst_ref=recv_c.at[j, blk, t],
                    send_sem=c_send.at[j, 0], recv_sem=c_recv.at[j, blk, t],
                    device_id=sibling, device_id_type=MESH,
                ).wait_recv()
        s_copy(j).start()

    mine = jnp.where(c == 0, GUIDANCE, 1.0 - GUIDANCE)
    theirs = 1.0 - mine

    def guide(j):
        s_copy(j).wait_recv()
        for blk in range(2):
            for t in range(4):
                g = mine * recv_c[j, blk, t].astype(F32) + theirs * sib_c[j, blk, t].astype(F32)
                gbuf[blk * 48 : blk * 48 + 48, t * HD : (t + 1) * HD] = g.astype(BF16)
        for t in range(4):
            w_copies[j * 4 + t].wait()

    def d_copy(n):
        return pltpu.make_async_remote_copy(
            src_ref=dsend.at[n], dst_ref=drecv.at[n],
            send_sem=d_send.at[n], recv_sem=d_recv.at[n],
            device_id=(c, s, 1 - xl), device_id_type=MESH,
        )

    def project(j):
        guide(j)
        for n in range(3):
            part = dot(gbuf[...], wv[j, :, n * 512 : (n + 1) * 512])
            if j > 0:
                part += acc[n]
            acc[n] = part
            if j == NJ - 1:
                dsend[n] = acc[n, pl.ds(pl.multiple_of((1 - xl) * 48, 16), 48), :].astype(BF16)
                d_copy(n).start()

    gather(0)
    forward(0)
    gather(1)
    attend(0)
    forward(1)
    gather(2)
    attend(1)
    forward(2)
    merge(0)
    attend(2)
    merge(1)
    share_out(0)
    project(0)
    merge(2)
    share_out(1)
    project(1)
    share_out(2)
    project(2)

    for n in range(3):
        d_copy(n).wait_recv()
        full = acc[n, pl.ds(pl.multiple_of(xl * 48, 16), 48), :] + drecv[n].astype(F32)
        o_ref[:, n * 512 : (n + 1) * 512] = full[0:ROWS].astype(BF16)

    for j in range(NJ):
        @pl.loop(0, NZ)
        def _(zz):
            @pl.when(jnp.logical_not(own(zz)))
            def _():
                a_copy(j, zz).wait_send()

            @pl.when(jnp.logical_not(c_own(zz)))
            def _():
                c_copy(j, zz).wait_send()

        for step in range(1, 4):
            q_copy(j, step).wait_send()
            for copy in m_copies(j, step):
                copy.wait_send()
        for way in range(2):
            kv_copy(j, way).wait_send()
            f_copy(j, way).wait_send()
        s_copy(j).wait_send()
    for n in range(3):
        d_copy(n).wait_send()


def shards(query, key, value, out_weight, table):
    vmem = pl.BlockSpec(memory_space=pltpu.VMEM)
    hbm = pl.BlockSpec(memory_space=pl.ANY)
    dma = pltpu.SemaphoreType.DMA
    return pl.pallas_call(
        kernel,
        out_shape=jax.ShapeDtypeStruct((ROWS, 1536), BF16),
        in_specs=[vmem, vmem, vmem, hbm, hbm],
        out_specs=vmem,
        scratch_shapes=[
            pltpu.VMEM((2, 40, HD), F32),
            pltpu.VMEM((2, 8, HD), F32),
            pltpu.VMEM((NJ, NZ, 112, HD), BF16),
            pltpu.VMEM((NJ, NZ, 112, HD), BF16),
            pltpu.VMEM((NJ, 4, TOK, HD), BF16),
            pltpu.VMEM((NJ, NY, 2, TOK, HD), BF16),
            pltpu.VMEM((HD, KS), BF16),
            pltpu.VMEM((NJ, QS, HD), BF16),
            pltpu.VMEM((NJ, 8, QS), F32),
            pltpu.VMEM((NJ, 4, TOK, HD), BF16),
            pltpu.VMEM((NJ, 4, 8, WIN), F32),
            pltpu.VMEM((WIN, HD), F32),
            pltpu.VMEM((NJ, NZ, 48, HD), BF16),
            pltpu.VMEM((NJ, 2, 4, 48, HD), BF16),
            pltpu.VMEM((NJ, 2, 4, 48, HD), BF16),
            pltpu.VMEM((96, 512), BF16),
            pltpu.VMEM((3, 96, 512), F32),
            pltpu.VMEM((3, 48, 512), BF16),
            pltpu.VMEM((3, 48, 512), BF16),
            pltpu.VMEM((NJ, 512, 1536), BF16),
            dma(()), dma((NJ, 4)),
            dma((NJ, NZ)), dma((NJ, NZ)),
            dma((NJ, 3)), dma((NJ, 3)),
            dma((NJ, 2)), dma((NJ, 2)),
            dma((NJ, 2)), dma((NJ, 2)),
            dma((NJ, 3)), dma((NJ, 3)),
            dma((NJ, 3)), dma((NJ, 3)),
            dma((NJ, NZ)), dma((NJ, 2, 4)),
            dma((NJ,)), dma((NJ,)),
            dma((3,)), dma((3,)),
        ],
        compiler_params=pltpu.CompilerParams(
            collective_id=0, has_side_effects=True, vmem_limit_bytes=48 * 1024 * 1024
        ),
        cost_estimate=pl.CostEstimate(flops=2_400_000_000, bytes_accessed=8_000_000, transcendentals=4_000_000),
    )(query, key, value, out_weight, table)


def solution(mesh):
    places = mesh.shape["seq"] * mesh.shape["blk"]
    call = jax.shard_map(
        shards,
        mesh=mesh,
        in_specs=(
            P("branch", ("seq", "blk"), None),
            P("branch", ("seq", "blk"), None),
            P("branch", ("seq", "blk"), None),
            P("blk", None),
            P(),
        ),
        out_specs=P(("seq", "blk"), "branch"),
        check_vma=False,
    )

    def run(query, key, value, out_weight):
        return call(query, key, value, out_weight, jnp.asarray(tables(places)))

    return run
```

time: 496 us -> 74 us (0.15)
  waiting for transfers between devices: 364 us -> 0 us
  Pallas kernels: 0 us -> 67.9 us
  local copies, waits for them, and re-layouts: 44.1 us -> 5.97 us
  matrix products: 31.7 us -> 0 us
  other arithmetic: 20.7 us -> 0 us
  blocking collectives: 19.7 us -> 0 us
  between operations: 13.9 us -> 0.01 us
    all_gather x2 -> x0, waiting for transfers between devices: 328 us -> none  [the longest x1 177 us: shards(): lax.all_gather(local_k, 'seq', axis=0, tiled=True)]
    pallas_call x0 -> x1, Pallas kernels: none -> 67.9 us  [shards(): pl.pallas_call(kernel, out_shape=jax.ShapeDtypeStruct((ROWS, 1536), BF16)...]
    all_gather x2 -> x0, local copies, waits for them, and re-layouts: 37.4 us -> none  [the longest x1 18.7 us: shards(): lax.all_gather(local_k, 'seq', axis=0, tiled=True)]
    unnamed x4 -> x0, waiting for transfers between devices: 34.7 us -> none
    dot_general x3 -> x0, matrix products: 31.7 us -> none  [the longest x1 13.1 us: make_step(): jnp.einsum('qhd,khd->hqk', q_heads, k_heads, preferred_element_type=jnp.f...]
    all_to_all x3 -> x0, blocking collectives: 19.7 us -> none  [the longest x1 7.04 us: shards(): lax.all_to_all(turned_k, 'blk', split_axis=1, concat_axis=0, tiled=True)]
    another operation x4 -> x0, other arithmetic: 10.4 us -> none  [the longest x2 5.49 us: rotate(): jnp.stack([first, second], axis=-1).reshape(count, -1).astype(jnp.bfloat16)]
    reduce_sum x1 -> x0, other arithmetic: 8.3 us -> none  [make_step(): total = jnp.sum(expo, axis=-1)]
  transfers between devices with their start and end apart: 4 -> 0, of which waited for: 4 -> 0; matrix products, arithmetic and copies ran while one was open for 9% -> 0% of each run, Pallas kernels for 0% -> 0%
where the time goes in v1:
time: 74 us; the launch traced here: 73.8 us
  Pallas kernels  67.9 us (92%)
  local copies, waits for them, and re-layouts  5.97 us (8%)
    pallas_call x1, Pallas kernels, shards(): pl.pallas_call(kernel, out_shape=jax.ShapeDtypeStruct((ROWS, 1536), BF16)...  67.9 us
    unnamed x9, local copies, waits for them, and re-layouts  5.97 us

profile of v1, /device:TPU:1, one launch (start us, length us, event | category | flops | bytes accessed | tf_op | source)
XLA Modules:
  0.0 73.8 jit_solution(18422481248414020378)
XLA Ops:
  0.0 0.0 copy-start
  0.0 2.5 %copy-done = f32[128,2,40,128]{3,2,1,0:T(8,128)S(1)} copy-done((f32[128,2,40,128]{3,2,1,0:T(8,128)S(1)}, f32[128,2,40,128]{3,2,1,0:T(8,128)}, u32[]{:S(2)}) %copy-start) | copy-done | bytes 5242904
  2.5 0.0 copy-start.1
  2.5 0.9 %copy-done.1 = bf16[1,36,3072]{2,1,0:T(8,128)(2,1)S(1)} copy-done((bf16[1,36,3072]{2,1,0:T(8,128)(2,1)S(1)}, bf16[1,36,3072]{2,1,0:T(8,128)(2,1)}, u32[]{:S(2)}) %copy-start.1) | copy-done | bytes 221208
  3.4 0.0 copy-start.2
  3.4 0.9 %copy-done.2 = bf16[1,36,3072]{2,1,0:T(8,128)(2,1)S(1)} copy-done((bf16[1,36,3072]{2,1,0:T(8,128)(2,1)S(1)}, bf16[1,36,3072]{2,1,0:T(8,128)(2,1)}, u32[]{:S(2)}) %copy-start.2) | copy-done | bytes 221208
  4.4 0.0 copy-start.3
  4.4 0.9 %copy-done.3 = bf16[1,36,3072]{2,1,0:T(8,128)(2,1)S(1)} copy-done((bf16[1,36,3072]{2,1,0:T(8,128)(2,1)S(1)}, bf16[1,36,3072]{2,1,0:T(8,128)(2,1)}, u32[]{:S(2)}) %copy-start.3) | copy-done | bytes 221208
  5.3 67.9 %shard_map.55 = bf16[36,1536]{1,0:T(8,128)(2,1)S(1)} custom-call(bf16[1,36,3072]{2,1,0:T(8,128)(2,1)S(1)} %copy-done.1, bf16[1,36,3072]{2,1,0:T(8,128)(2,1)S(1)} %copy-done.2, bf16[1,36,3072]{2,1,0:T(8,128)(2,1)S(1)} %copy-done.3, bf16[1536,3072]{1,0:T(8,128)(2,1)} %w_ref.1, f32[128,2,40,128]{3,2,1,0:T(8,128)S(1)} %copy-done), custom_call_target="tpu_custom_call" | custom-call | flops 2400000000 | bytes 8000000 | tf_op jit(solution)/shard_map/pallas_call | solution.py:437
  73.2 0.7 copy.7
Async XLA Ops:
  0.0 2.5 %copy-start = (f32[128,2,40,128]{3,2,1,0:T(8,128)S(1)}, f32[128,2,40,128]{3,2,1,0:T(8,128)}, u32[]{:S(2)}) copy-start(f32[128,2,40,128]{3,2,1,0:T(8,128)} %constant.2.clone.tab_ref) | copy-start | bytes 15728644
  2.5 0.9 %copy-start.1 = (bf16[1,36,3072]{2,1,0:T(8,128)(2,1)S(1)}, bf16[1,36,3072]{2,1,0:T(8,128)(2,1)}, u32[]{:S(2)}) copy-start(bf16[1,36,3072]{2,1,0:T(8,128)(2,1)} %q_ref.1) | copy-start | bytes 663556
  3.4 0.9 %copy-start.2 = (bf16[1,36,3072]{2,1,0:T(8,128)(2,1)S(1)}, bf16[1,36,3072]{2,1,0:T(8,128)(2,1)}, u32[]{:S(2)}) copy-start(bf16[1,36,3072]{2,1,0:T(8,128)(2,1)} %k_ref.1) | copy-start | bytes 663556
  4.4 0.9 %copy-start.3 = (bf16[1,36,3072]{2,1,0:T(8,128)(2,1)S(1)}, bf16[1,36,3072]{2,1,0:T(8,128)(2,1)}, u32[]{:S(2)}) copy-start(bf16[1,36,3072]{2,1,0:T(8,128)(2,1)} %v_ref.1) | copy-start | bytes 663556

commit v2 on v1

v2 whole, which is shorter than its diff:
```python
import functools

import jax
import jax.numpy as jnp
import numpy as np
from jax import lax
from jax.experimental import pallas as pl
from jax.experimental.pallas import tpu as pltpu
from jax.sharding import PartitionSpec as P

HD = 128
GRIDW = 256
GUIDANCE = 4.0
F32 = jnp.float32
BF16 = jnp.bfloat16
MESH = pl.DeviceIdType.MESH

NJ = 3
NZ = 8
NY = 4
ROWS = 36
MAIN = 32
REM = ROWS - MAIN
TOK = NZ * ROWS
QS = 4 * TOK
KS = NY * TOK
PART = (0, 48, 80, 112)
SCALE = float(HD**-0.5 / np.log(2.0))


def tables(places):
    time_dim = HD // 8
    side_dim = (HD - time_dim) // 2
    index = np.arange(side_dim // 2).astype(np.float32)
    freq = np.power(np.float32(10000.0), -2.0 * index / side_dim).astype(np.float32)
    at = np.arange(places * ROWS)
    row = (at // GRIDW).astype(np.float32)[:, None] * freq[None, :]
    col = (at % GRIDW).astype(np.float32)[:, None] * freq[None, :]
    still = np.zeros((places * ROWS, time_dim // 2), np.float32)
    angle = np.repeat(np.concatenate([still, row, col], axis=1), 2, axis=1).astype(np.float64)
    sign = np.where(np.arange(HD) % 2 == 0, -1.0, 1.0)
    both = np.stack([np.cos(angle), np.sin(angle) * sign]).astype(np.float32)
    out = np.zeros((places, 2, 40, HD), np.float32)
    out[:, :, :ROWS] = both.reshape(2, places, ROWS, HD).transpose(1, 0, 2, 3)
    return out


def turn(x, cos, sin):
    even = lax.broadcasted_iota(jnp.int32, x.shape, 1) % 2 == 0
    swapped = jnp.where(even, pltpu.roll(x, HD - 1, 1), pltpu.roll(x, 1, 1))
    return x * cos + swapped * sin


def pick(shape, source):
    row = lax.broadcasted_iota(jnp.int32, shape, 0)
    col = lax.broadcasted_iota(jnp.int32, shape, 1)
    return jnp.where(col == source(row), 1.0, 0.0).astype(BF16)


def outward(i):
    return jnp.where(i % 2 == 1, 4 - (i + 1) // 2, 4 + i // 2)


def dot(a, b):
    return jnp.dot(a, b, preferred_element_type=F32)


def kernel(
    q_hbm, k_hbm, v_hbm, w_ref, tab_ref, o_ref,
    q_ref, k_ref, v_ref, tab, rtab, send_a, recv_a, qall, kv, vt, obuf, pst, mo, mst, wt, cbuf,
    recv_c, sib_c, gbuf, acc, dsend, drecv, dsend4, drecv4, wv,
    in_sem, w_sem, a_send, a_recv, q_send, q_recv, y_send, y_recv, f_send, f_recv,
    m_send, m_recv, n_send, n_recv, c_send, c_recv, s_send, s_recv, d_send, d_recv,
):
    c = lax.axis_index("branch")
    s = lax.axis_index("seq")
    xl = lax.axis_index("blk")
    xh = s // 32
    y = (s // 8) % 4
    z = s % 8
    place = s * 2 + xl
    slot = xl * 2 + c

    def far(zz, blk):
        return (xh, (c * 4 + y) * 8 + zz, blk)

    def ring(step):
        return (c, (xh * 4 + (y + step) % 4) * 8 + z, xl)

    def near(step):
        device = ((c + step) % 2, s, (xl + step // 2) % 2)
        return device, device[2] * 2 + device[0]

    barrier = pltpu.get_barrier_semaphore()

    @pl.loop(0, NZ)
    def _(zz):
        for blk in range(2):
            @pl.when(jnp.logical_not((xh == c) & (zz == z) & (xl == blk)))
            def _():
                pl.semaphore_signal(barrier, inc=1, device_id=far(zz, blk), device_id_type=MESH)

    for step in range(1, 4):
        pl.semaphore_signal(barrier, inc=1, device_id=ring(step), device_id_type=MESH)
        pl.semaphore_signal(barrier, inc=1, device_id=near(step)[0], device_id_type=MESH)

    loads = [
        pltpu.make_async_copy(src, dst, in_sem.at[i])
        for i, (src, dst) in enumerate(
            ((tab_ref.at[place], tab), (k_hbm.at[0], k_ref), (q_hbm.at[0], q_ref), (v_hbm.at[0], v_ref))
        )
    ]
    for load in loads:
        load.start()
    w_copies = []
    for j in range(NJ):
        for t in range(4):
            w_copies.append(
                pltpu.make_async_copy(
                    w_ref.at[pl.ds((t * NJ + j) * HD, HD), pl.ds(pl.multiple_of(c * 1536, 1536), 1536)],
                    wv.at[j, pl.ds(t * HD, HD)],
                    w_sem.at[j, t],
                )
            )
            w_copies[-1].start()

    def own(zz):
        return (xh == c) & (zz == z)

    def a_copy(j, p, zz):
        rows = pl.ds(PART[p], PART[p + 1] - PART[p])
        return pltpu.make_async_remote_copy(
            src_ref=send_a.at[j, zz, rows], dst_ref=recv_a.at[j, z, rows],
            send_sem=a_send.at[j, p, zz], recv_sem=a_recv.at[j, p, z],
            device_id=far(zz, xl), device_id_type=MESH,
        )

    def a_local(j, p):
        rows = pl.ds(PART[p], PART[p + 1] - PART[p])
        return pltpu.make_async_copy(send_a.at[j, z, rows], recv_a.at[j, z, rows], a_recv.at[j, p, z])

    def a_arrival(j, p, zz):
        rows = pl.ds(PART[p], PART[p + 1] - PART[p])
        return pltpu.make_async_remote_copy(
            src_ref=send_a.at[j, zz, rows], dst_ref=recv_a.at[j, zz, rows],
            send_sem=a_send.at[j, p, zz], recv_sem=a_recv.at[j, p, zz],
            device_id=far(zz, xl), device_id_type=MESH,
        )

    for load in loads:
        load.wait()
    rtab[0, 0:4] = tab[0, 32:36] * SCALE
    rtab[0, 4:8] = tab[0, 32:36]
    rtab[1, 0:4] = tab[1, 32:36] * SCALE
    rtab[1, 4:8] = tab[1, 32:36]

    def prepare(j):
        @pl.loop(0, NZ)
        def _(zz):
            cols = pl.ds(pl.multiple_of((zz * NJ + j) * HD, HD), HD)
            cos, sin = tab[0, 0:MAIN], tab[1, 0:MAIN]
            q = turn(q_ref[0:MAIN, cols].astype(F32), cos * SCALE, sin * SCALE)
            k = turn(k_ref[0:MAIN, cols].astype(F32), cos, sin)
            send_a[j, zz, 0:32] = k.astype(BF16)
            send_a[j, zz, 48:80] = v_ref[0:MAIN, cols]
            send_a[j, zz, 80:112] = q.astype(BF16)
            qk = jnp.concatenate(
                [q_ref[MAIN:ROWS, cols].astype(F32), k_ref[MAIN:ROWS, cols].astype(F32)], axis=0
            )
            v4 = v_ref[MAIN:ROWS, cols].astype(F32)
            rest = jnp.concatenate([turn(qk, rtab[0], rtab[1]), v4, jnp.zeros_like(v4)], axis=0)
            send_a[j, zz, 32:48] = rest.astype(BF16)

    def depart(j, p):
        @pl.loop(0, NZ)
        def _(i):
            zz = (z + outward(i)) % NZ

            @pl.when(own(zz))
            def _():
                a_local(j, p).start()

            @pl.when(jnp.logical_not(own(zz)))
            def _():
                a_copy(j, p, zz).start()

    def y_copy(j, p, way):
        return pltpu.make_async_remote_copy(
            src_ref=kv.at[j, 0, p], dst_ref=kv.at[j, 1 + way, p],
            send_sem=y_send.at[j, p, way], recv_sem=y_recv.at[j, p, way],
            device_id=ring(1 if way == 0 else 3), device_id_type=MESH,
        )

    def f_copy(j, p, way):
        rows = pl.ds(way * 144, 144)
        return pltpu.make_async_remote_copy(
            src_ref=kv.at[j, 1 + way, p, rows], dst_ref=kv.at[j, 3, p, rows],
            send_sem=f_send.at[j, p, way], recv_sem=f_recv.at[j, p, way],
            device_id=ring(1 if way == 0 else 3), device_id_type=MESH,
        )

    def q_copy(j, step):
        which = near(2)[1] if step == 3 else slot
        return pltpu.make_async_remote_copy(
            src_ref=qall.at[j, which], dst_ref=qall.at[j, which],
            send_sem=q_send.at[j, step - 1], recv_sem=q_recv.at[j, step - 1],
            device_id=near(2 if step == 2 else 1)[0], device_id_type=MESH,
        )

    def gather(j, p):
        for zz in range(NZ):
            a_arrival(j, p, zz).wait_recv()
        if p == 0:
            for zz in range(NZ):
                kv[j, 0, 0, zz * 32 : zz * 32 + 32] = recv_a[j, zz, 0:32]
            rest = recv_a[j, :, 32:48, :].reshape(NZ * 16, HD)
            order = pick((96, 128), lambda r: (r % 32) // 4 * 16 + r // 32 * 4 + r % 4)
            rest = dot(order, rest).astype(BF16)
            kv[j, 0, 0, 256:288] = rest[32:64]
            kv[j, 0, 1, 256:288] = rest[64:96]
            qall[j, slot, 256:288] = rest[0:32]
        elif p == 1:
            for zz in range(NZ):
                kv[j, 0, 1, zz * 32 : zz * 32 + 32] = recv_a[j, zz, 48:80]
        else:
            for zz in range(NZ):
                qall[j, slot, zz * 32 : zz * 32 + 32] = recv_a[j, zz, 80:112]
        if p < 2:
            for way in range(2):
                y_copy(j, p, way).start()
        else:
            for step in (2, 1):
                q_copy(j, step).start()

    def forward(j, p):
        if p < 2:
            for way in range(2):
                y_copy(j, p, way).wait_recv()
                f_copy(j, p, way).start()
        else:
            q_copy(j, 2).wait_recv()
            q_copy(j, 3).start()

    def m_copies(j, step):
        device, other = near(step)
        return (
            pltpu.make_async_remote_copy(
                src_ref=obuf.at[j, pl.ds(pl.multiple_of(other * TOK, 32), TOK)], dst_ref=mo.at[j, slot],
                send_sem=m_send.at[j, step - 1], recv_sem=m_recv.at[j, step - 1],
                device_id=device, device_id_type=MESH,
            ),
            pltpu.make_async_remote_copy(
                src_ref=pst.at[j, other], dst_ref=mst.at[j, slot],
                send_sem=n_send.at[j, step - 1], recv_sem=n_recv.at[j, step - 1],
                device_id=device, device_id_type=MESH,
            ),
        )

    def m_arrivals(j, step):
        device, other = near(step)
        return (
            pltpu.make_async_remote_copy(
                src_ref=mo.at[j, slot], dst_ref=mo.at[j, other],
                send_sem=m_send.at[j, step - 1], recv_sem=m_recv.at[j, step - 1],
                device_id=device, device_id_type=MESH,
            ),
            pltpu.make_async_remote_copy(
                src_ref=mst.at[j, slot], dst_ref=mst.at[j, other],
                send_sem=n_send.at[j, step - 1], recv_sem=n_recv.at[j, step - 1],
                device_id=device, device_id_type=MESH,
            ),
        )

    def attend(j):
        q_copy(j, 1).wait_recv()
        q_copy(j, 3).wait_recv()
        for p in range(2):
            for way in range(2):
                f_copy(j, p, way).wait_recv()
        for t in range(NY):
            vt[:, t * TOK : (t + 1) * TOK] = kv[j, t, 1].astype(F32).T.astype(BF16)
        queries = qall[j].reshape(QS, HD)
        keys = kv[j, :, 0].reshape(KS, HD)
        scores = lax.dot_general(keys, queries, (((1,), (1,)), ((), ())), preferred_element_type=F32)
        top = jnp.max(scores, axis=0, keepdims=True)
        expo = jnp.exp2(scores - top)
        total = jnp.sum(expo, axis=0, keepdims=True)
        mixed = dot(vt[...], expo.astype(BF16)) / total
        obuf[j] = mixed.T.astype(BF16)
        for i in range(4):
            for r in range(3):
                lanes = slice((2 * i + r) * HD, (2 * i + r + 1) * HD)
                pst[j, i, r : r + 1, :] = top[:, lanes]
                pst[j, i, 3 + r : 4 + r, :] = total[:, lanes]
            pst[j, i, 6:8, :] = jnp.zeros((2, HD), F32)
        for step in (3, 2, 1):
            for copy in m_copies(j, step):
                copy.start()
        mo[j, slot] = obuf[j, pl.ds(pl.multiple_of(slot * TOK, 32), TOK), :]
        mst[j, slot] = pst[j, slot]

    def c_copy(j, zz):
        return pltpu.make_async_remote_copy(
            src_ref=cbuf.at[j, zz], dst_ref=recv_c.at[j, xl, z % 4],
            send_sem=c_send.at[j, zz], recv_sem=c_recv.at[j, xl, z % 4],
            device_id=far(zz, z // 4), device_id_type=MESH,
        )

    def c_own(zz):
        return (xh == c) & (zz == z) & (z // 4 == xl)

    def merge(j):
        for step in range(1, 4):
            for copy in m_arrivals(j, step):
                copy.wait_recv()
        tops = [mst[j, i, 0:3, :] for i in range(4)]
        top = jnp.maximum(jnp.maximum(tops[0], tops[1]), jnp.maximum(tops[2], tops[3]))
        parts = [mst[j, i, 3:6, :] * jnp.exp2(tops[i] - top) for i in range(4)]
        total = (parts[0] + parts[1]) + (parts[2] + parts[3])
        parts = [p / total for p in parts]
        for r in range(3):
            rows = jnp.concatenate([p[r : r + 1] for p in parts] + [jnp.zeros((124, HD), F32)], axis=0)
            wt[r * HD : (r + 1) * HD] = rows.T
        share = wt[pl.ds(pl.multiple_of(slot * 32, 32), TOK), :]
        mixed = share[:, 0:1] * mo[j, 0].astype(F32)
        for i in range(1, 4):
            mixed += share[:, i : i + 1] * mo[j, i].astype(F32)
        mixed = mixed.astype(BF16)
        order = pick((128, 32), lambda r: jnp.where(r % 16 < 4, r // 16 * 4 + r % 16, -1))
        rest = dot(order, mixed[256:288]).astype(BF16)
        for zz in range(NZ):
            cbuf[j, zz, 0:32] = mixed[zz * 32 : zz * 32 + 32]
            cbuf[j, zz, 32:48] = rest[zz * 16 : zz * 16 + 16]

        @pl.loop(0, NZ)
        def _(i):
            zz = (z + outward(i)) % NZ

            @pl.when(c_own(zz))
            def _():
                pltpu.make_async_copy(cbuf.at[j, z], recv_c.at[j, xl, z % 4], c_recv.at[j, xl, z % 4]).start()

            @pl.when(jnp.logical_not(c_own(zz)))
            def _():
                c_copy(j, zz).start()

    sibling = (1 - c, s, xl)

    def s_copy(j):
        return pltpu.make_async_remote_copy(
            src_ref=recv_c.at[j], dst_ref=sib_c.at[j],
            send_sem=s_send.at[j], recv_sem=s_recv.at[j],
            device_id=sibling, device_id_type=MESH,
        )

    def share_out(j):
        for blk in range(2):
            for t in range(4):
                pltpu.make_async_remote_copy(
                    src_ref=cbuf.at[j, 0], dst_ref=recv_c.at[j, blk, t],
                    send_sem=c_send.at[j, 0], recv_sem=c_recv.at[j, blk, t],
                    device_id=sibling, device_id_type=MESH,
                ).wait_recv()
        s_copy(j).start()

    mine = jnp.where(c == 0, GUIDANCE, 1.0 - GUIDANCE)
    theirs = 1.0 - mine

    def d_copy(n):
        src, dst = (dsend.at[n], drecv.at[n]) if n < 3 else (dsend4, drecv4)
        return pltpu.make_async_remote_copy(
            src_ref=src, dst_ref=dst,
            send_sem=d_send.at[n], recv_sem=d_recv.at[n],
            device_id=(c, s, 1 - xl), device_id_type=MESH,
        )

    def project(j):
        s_copy(j).wait_recv()
        for blk in range(2):
            for t in range(4):
                g = mine * recv_c[j, blk, t].astype(F32) + theirs * sib_c[j, blk, t].astype(F32)
                gbuf[blk * 48 : blk * 48 + 48, t * HD : (t + 1) * HD] = g.astype(BF16)
        for t in range(4):
            w_copies[j * 4 + t].wait()
        rest = []
        for n in range(3):
            part = dot(gbuf[...], wv[j, :, n * 512 : (n + 1) * 512])
            if j > 0:
                part += acc[n]
            acc[n] = part
            if j == NJ - 1:
                other = pl.multiple_of((1 - xl) * 48, 16)
                dsend[n] = acc[n, pl.ds(other, MAIN), :].astype(BF16)
                d_copy(n).start()
                rest.append(acc[n, pl.ds(other + MAIN, 8), :][0:REM])
        if j == NJ - 1:
            dsend4[...] = jnp.concatenate(rest + [jnp.zeros_like(rest[0])], axis=0).astype(BF16)
            d_copy(3).start()

    prepare(0)
    pl.semaphore_wait(barrier, jnp.where(xh == c, 21, 22))
    depart(0, 0)
    depart(0, 1)
    depart(0, 2)
    prepare(1)
    depart(1, 0)
    depart(1, 1)
    depart(1, 2)
    prepare(2)
    depart(2, 0)
    depart(2, 1)
    depart(2, 2)
    gather(0, 0)
    gather(0, 1)
    gather(0, 2)
    forward(0, 0)
    forward(0, 1)
    gather(1, 0)
    forward(0, 2)
    gather(1, 1)
    gather(1, 2)
    forward(1, 0)
    attend(0)
    forward(1, 1)
    gather(2, 0)
    gather(2, 1)
    forward(1, 2)
    gather(2, 2)
    forward(2, 0)
    attend(1)
    forward(2, 1)
    forward(2, 2)
    merge(0)
    attend(2)
    merge(1)
    share_out(0)
    project(0)
    merge(2)
    share_out(1)
    project(1)
    share_out(2)
    project(2)

    mine_at = pl.multiple_of(xl * 48, 16)
    for n in range(3):
        d_copy(n).wait_recv()
        full = acc[n, pl.ds(mine_at, MAIN), :] + drecv[n].astype(F32)
        o_ref[0:MAIN, n * 512 : (n + 1) * 512] = full.astype(BF16)
    d_copy(3).wait_recv()
    rest = drecv4[...].astype(F32)
    for n in range(3):
        full = acc[n, pl.ds(mine_at + MAIN, 8), :][0:REM] + rest[n * REM : (n + 1) * REM]
        o_ref[MAIN:ROWS, n * 512 : (n + 1) * 512] = full.astype(BF16)

    for j in range(NJ):
        @pl.loop(0, NZ)
        def _(zz):
            @pl.when(jnp.logical_not(own(zz)))
            def _():
                for p in range(3):
                    a_copy(j, p, zz).wait_send()

            @pl.when(jnp.logical_not(c_own(zz)))
            def _():
                c_copy(j, zz).wait_send()

        for step in range(1, 4):
            q_copy(j, step).wait_send()
            for copy in m_copies(j, step):
                copy.wait_send()
        for p in range(2):
            for way in range(2):
                y_copy(j, p, way).wait_send()
                f_copy(j, p, way).wait_send()
        s_copy(j).wait_send()
    for n in range(4):
        d_copy(n).wait_send()


def shards(query, key, value, out_weight, table):
    hbm = pl.BlockSpec(memory_space=pl.ANY)
    dma = pltpu.SemaphoreType.DMA
    return pl.pallas_call(
        kernel,
        out_shape=jax.ShapeDtypeStruct((ROWS, 1536), BF16),
        in_specs=[hbm] * 5,
        out_specs=pl.BlockSpec(memory_space=pltpu.VMEM),
        scratch_shapes=[
            pltpu.VMEM((ROWS, 3072), BF16),
            pltpu.VMEM((ROWS, 3072), BF16),
            pltpu.VMEM((ROWS, 3072), BF16),
            pltpu.VMEM((2, 40, HD), F32),
            pltpu.VMEM((2, 8, HD), F32),
            pltpu.VMEM((NJ, NZ, 112, HD), BF16),
            pltpu.VMEM((NJ, NZ, 112, HD), BF16),
            pltpu.VMEM((NJ, 4, TOK, HD), BF16),
            pltpu.VMEM((NJ, NY, 2, TOK, HD), BF16),
            pltpu.VMEM((HD, KS), BF16),
            pltpu.VMEM((NJ, QS, HD), BF16),
            pltpu.VMEM((NJ, 4, 8, HD), F32),
            pltpu.VMEM((NJ, 4, TOK, HD), BF16),
            pltpu.VMEM((NJ, 4, 8, HD), F32),
            pltpu.VMEM((3 * HD, HD), F32),
            pltpu.VMEM((NJ, NZ, 48, HD), BF16),
            pltpu.VMEM((NJ, 2, 4, 48, HD), BF16),
            pltpu.VMEM((NJ, 2, 4, 48, HD), BF16),
            pltpu.VMEM((96, 512), BF16),
            pltpu.VMEM((3, 96, 512), F32),
            pltpu.VMEM((3, 32, 512), BF16),
            pltpu.VMEM((3, 32, 512), BF16),
            pltpu.VMEM((16, 512), BF16),
            pltpu.VMEM((16, 512), BF16),
            pltpu.VMEM((NJ, 512, 1536), BF16),
            dma((4,)), dma((NJ, 4)),
            dma((NJ, 3, NZ)), dma((NJ, 3, NZ)),
            dma((NJ, 3)), dma((NJ, 3)),
            dma((NJ, 2, 2)), dma((NJ, 2, 2)),
            dma((NJ, 2, 2)), dma((NJ, 2, 2)),
            dma((NJ, 3)), dma((NJ, 3)),
            dma((NJ, 3)), dma((NJ, 3)),
            dma((NJ, NZ)), dma((NJ, 2, 4)),
            dma((NJ,)), dma((NJ,)),
            dma((4,)), dma((4,)),
        ],
        compiler_params=pltpu.CompilerParams(
            collective_id=0, has_side_effects=True, vmem_limit_bytes=60 * 1024 * 1024
        ),
        cost_estimate=pl.CostEstimate(flops=2_400_000_000, bytes_accessed=8_000_000, transcendentals=4_000_000),
    )(query, key, value, out_weight, table)


def solution(mesh):
    places = mesh.shape["seq"] * mesh.shape["blk"]
    call = jax.shard_map(
        shards,
        mesh=mesh,
        in_specs=(
            P("branch", ("seq", "blk"), None),
            P("branch", ("seq", "blk"), None),
            P("branch", ("seq", "blk"), None),
            P("blk", None),
            P(),
        ),
        out_specs=P(("seq", "blk"), "branch"),
        check_vma=False,
    )

    def run(query, key, value, out_weight):
        return call(query, key, value, out_weight, jnp.asarray(tables(places)))

    return run
```

time: 74 us -> 63.4 us (0.86)
  Pallas kernels: 67.9 us -> 61.8 us
  local copies, waits for them, and re-layouts: 5.97 us -> 1.56 us
    pallas_call x1, Pallas kernels: 67.9 us -> 61.8 us  [shards(): pl.pallas_call(kernel, out_shape=jax.ShapeDtypeStruct((ROWS, 1536), BF16)...]
    unnamed x9 -> x1, local copies, waits for them, and re-layouts: 5.97 us -> 1.56 us
where the time goes in v2:
time: 63.4 us
  Pallas kernels  61.8 us (97%)
  local copies, waits for them, and re-layouts  1.56 us (2%)
    pallas_call x1, Pallas kernels, shards(): pl.pallas_call(kernel, out_shape=jax.ShapeDtypeStruct((ROWS, 1536), BF16)...  61.8 us
    unnamed x1, local copies, waits for them, and re-layouts  1.56 us

profile of v2, /device:TPU:1, one launch (start us, length us, event | category | flops | bytes accessed | tf_op | source)
XLA Modules:
  0.0 63.4 jit_solution(6469001271773307685)
XLA Ops:
  0.0 61.8 %shard_map.55 = bf16[36,1536]{1,0:T(8,128)(2,1)} custom-call(bf16[1,36,3072]{2,1,0:T(8,128)(2,1)} %q_hbm.1, bf16[1,36,3072]{2,1,0:T(8,128)(2,1)} %k_hbm.1, bf16[1,36,3072]{2,1,0:T(8,128)(2,1)} %v_hbm.1, bf16[1536,3072]{1,0:T(8,128)(2,1)} %w_ref.1, f32[128,2,40,128]{3,2,1,0:T(8,128)} %constant.2.clone.tab_ref), custom_call_target="tpu_custom_call" | custom-call | flops 2400000000 | bytes 8000000 | tf_op jit(solution)/shard_map/pallas_call | solution.py:483
  61.8 1.6 %copy.7 = bf16[36,1536]{1,0:T(8,128)(2,1)} copy(bf16[36,1536]{1,0:T(8,128)(2,1)} %shard_map.55) | data formatting | bytes 221184

commit v3 on v2

--- a/solution.py
+++ b/solution.py
@@ -91,6 +91,15 @@
         device = ((c + step) % 2, s, (xl + step // 2) % 2)
         return device, device[2] * 2 + device[0]
 
+    loads = [
+        pltpu.make_async_copy(src, dst, in_sem.at[i])
+        for i, (src, dst) in enumerate(
+            ((tab_ref.at[place], tab), (k_hbm.at[0], k_ref), (q_hbm.at[0], q_ref), (v_hbm.at[0], v_ref))
+        )
+    ]
+    for load in loads:
+        load.start()
+
     barrier = pltpu.get_barrier_semaphore()
 
     @pl.loop(0, NZ)
@@ -104,14 +113,6 @@
         pl.semaphore_signal(barrier, inc=1, device_id=ring(step), device_id_type=MESH)
         pl.semaphore_signal(barrier, inc=1, device_id=near(step)[0], device_id_type=MESH)
 
-    loads = [
-        pltpu.make_async_copy(src, dst, in_sem.at[i])
-        for i, (src, dst) in enumerate(
-            ((tab_ref.at[place], tab), (k_hbm.at[0], k_ref), (q_hbm.at[0], q_ref), (v_hbm.at[0], v_ref))
-        )
-    ]
-    for load in loads:
-        load.start()
     w_copies = []
     for j in range(NJ):
         for t in range(4):
@@ -122,7 +123,10 @@
                     w_sem.at[j, t],
                 )
             )
-            w_copies[-1].start()
+
+    def weights(j):
+        for t in range(4):
+            w_copies[j * 4 + t].start()
 
     def own(zz):
         return (xh == c) & (zz == z)
@@ -271,6 +275,22 @@
             ),
         )
 
+    def attend_rows(j, first, count):
+        queries = qall[j, pl.ds(first, count)].reshape(count * TOK, HD)
+        keys = kv[j, :, 0].reshape(KS, HD)
+        scores = lax.dot_general(keys, queries, (((1,), (1,)), ((), ())), preferred_element_type=F32)
+        top = jnp.max(scores, axis=0, keepdims=True)
+        expo = jnp.exp2(scores - top)
+        total = jnp.sum(expo, axis=0, keepdims=True)
+        mixed = dot(vt[...], expo.astype(BF16)) / total
+        obuf[j, pl.ds(pl.multiple_of(first * TOK, 32), count * TOK)] = mixed.T.astype(BF16)
+        for i in range(count):
+            for r in range(3):
+                lanes = slice((2 * i + r) * HD, min((2 * i + r + 1) * HD, count * TOK))
+                wide = slice(0, lanes.stop - lanes.start)
+                pst[j, first + i, r : r + 1, wide] = top[:, lanes]
+                pst[j, first + i, 3 + r : 4 + r, wide] = total[:, lanes]
+
     def attend(j):
         q_copy(j, 1).wait_recv()
         q_copy(j, 3).wait_recv()
@@ -279,23 +299,18 @@
                 f_copy(j, p, way).wait_recv()
         for t in range(NY):
             vt[:, t * TOK : (t + 1) * TOK] = kv[j, t, 1].astype(F32).T.astype(BF16)
-        queries = qall[j].reshape(QS, HD)
-        keys = kv[j, :, 0].reshape(KS, HD)
-        scores = lax.dot_general(keys, queries, (((1,), (1,)), ((), ())), preferred_element_type=F32)
-        top = jnp.max(scores, axis=0, keepdims=True)
-        expo = jnp.exp2(scores - top)
-        total = jnp.sum(expo, axis=0, keepdims=True)
-        mixed = dot(vt[...], expo.astype(BF16)) / total
-        obuf[j] = mixed.T.astype(BF16)
-        for i in range(4):
-            for r in range(3):
-                lanes = slice((2 * i + r) * HD, (2 * i + r + 1) * HD)
-                pst[j, i, r : r + 1, :] = top[:, lanes]
-                pst[j, i, 3 + r : 4 + r, :] = total[:, lanes]
-            pst[j, i, 6:8, :] = jnp.zeros((2, HD), F32)
-        for step in (3, 2, 1):
+        pst[j] = jnp.ones((4, 8, HD), F32)
+        if j < NJ - 1:
+            attend_rows(j, 0, 4)
+        else:
+            attend_rows(j, (1 - xl) * 2, 2)
+        for step in (3, 2):
             for copy in m_copies(j, step):
                 copy.start()
+        if j == NJ - 1:
+            attend_rows(j, xl * 2, 2)
+        for copy in m_copies(j, 1):
+            copy.start()
         mo[j, slot] = obuf[j, pl.ds(pl.multiple_of(slot * TOK, 32), TOK), :]
         mst[j, slot] = pst[j, slot]
 
@@ -321,7 +336,8 @@
         for r in range(3):
             rows = jnp.concatenate([p[r : r + 1] for p in parts] + [jnp.zeros((124, HD), F32)], axis=0)
             wt[r * HD : (r + 1) * HD] = rows.T
-        share = wt[pl.ds(pl.multiple_of(slot * 32, 32), TOK), :]
+        at = slot if j < NJ - 1 else c
+        share = wt[pl.ds(pl.multiple_of(at * 32, 32), TOK), :]
         mixed = share[:, 0:1] * mo[j, 0].astype(F32)
         for i in range(1, 4):
             mixed += share[:, i : i + 1] * mo[j, i].astype(F32)
@@ -430,8 +446,11 @@
     attend(1)
     forward(2, 1)
     forward(2, 2)
+    weights(0)
     merge(0)
     attend(2)
+    weights(1)
+    weights(2)
     merge(1)
     share_out(0)
     project(0)
@@ -482,7 +501,7 @@
     dma = pltpu.SemaphoreType.DMA
     return pl.pallas_call(
         kernel,
-        out_shape=jax.ShapeDtypeStruct((ROWS, 1536), BF16),
+        out_shape=pltpu.VMEM((ROWS, 1536), BF16),
         in_specs=[hbm] * 5,
         out_specs=pl.BlockSpec(memory_space=pltpu.VMEM),
         scratch_shapes=[

time: 63.4 us -> 59.7 us (0.942)
  Pallas kernels: 61.8 us -> 58.9 us
  local copies, waits for them, and re-layouts: 1.56 us -> 0.65 us
    pallas_call x1, Pallas kernels: 61.8 us -> 58.9 us  [shards(): pl.pallas_call(kernel, out_shape=pltpu.VMEM((ROWS, 1536), BF16), in_specs...]
    unnamed x1, local copies, waits for them, and re-layouts: 1.56 us -> 0.65 us
where the time goes in v3:
time: 59.7 us; the launch traced here: 59.6 us
  Pallas kernels  58.9 us (99%)
  local copies, waits for them, and re-layouts  0.65 us (1%)
    pallas_call x1, Pallas kernels, shards(): pl.pallas_call(kernel, out_shape=pltpu.VMEM((ROWS, 1536), BF16), in_specs...  58.9 us

profile of v3, /device:TPU:1, one launch (start us, length us, event | category | flops | bytes accessed | tf_op | source)
XLA Modules:
  0.0 59.6 jit_solution(10501343314299485524)
XLA Ops:
  0.0 58.9 %shard_map.55 = bf16[36,1536]{1,0:T(8,128)(2,1)S(1)} custom-call(bf16[1,36,3072]{2,1,0:T(8,128)(2,1)} %q_hbm.1, bf16[1,36,3072]{2,1,0:T(8,128)(2,1)} %k_hbm.1, bf16[1,36,3072]{2,1,0:T(8,128)(2,1)} %v_hbm.1, bf16[1536,3072]{1,0:T(8,128)(2,1)} %w_ref.1, f32[128,2,40,128]{3,2,1,0:T(8,128)} %constant.2.clone.tab_ref), custom_call_target="tpu_custom_call" | custom-call | flops 2400000000 | bytes 8000000 | tf_op jit(solution)/shard_map/pallas_call | solution.py:502
  58.9 0.7 %copy.7 = bf16[36,1536]{1,0:T(8,128)(2,1)} copy(bf16[36,1536]{1,0:T(8,128)(2,1)S(1)} %shard_map.55) | data formatting | bytes 221184

commit v4 on v3

--- a/solution.py
+++ b/solution.py
@@ -69,7 +69,7 @@
     q_hbm, k_hbm, v_hbm, w_ref, tab_ref, o_ref,
     q_ref, k_ref, v_ref, tab, rtab, send_a, recv_a, qall, kv, vt, obuf, pst, mo, mst, wt, cbuf,
     recv_c, sib_c, gbuf, acc, dsend, drecv, dsend4, drecv4, wv,
-    in_sem, w_sem, a_send, a_recv, q_send, q_recv, y_send, y_recv, f_send, f_recv,
+    in_sem, w_sem, a_send, a_recv, q_send, q_recv, y_send, y_recv,
     m_send, m_recv, n_send, n_recv, c_send, c_recv, s_send, s_recv, d_send, d_recv,
 ):
     c = lax.axis_index("branch")
@@ -192,23 +192,14 @@
         return pltpu.make_async_remote_copy(
             src_ref=kv.at[j, 0, p], dst_ref=kv.at[j, 1 + way, p],
             send_sem=y_send.at[j, p, way], recv_sem=y_recv.at[j, p, way],
-            device_id=ring(1 if way == 0 else 3), device_id_type=MESH,
-        )
-
-    def f_copy(j, p, way):
-        rows = pl.ds(way * 144, 144)
-        return pltpu.make_async_remote_copy(
-            src_ref=kv.at[j, 1 + way, p, rows], dst_ref=kv.at[j, 3, p, rows],
-            send_sem=f_send.at[j, p, way], recv_sem=f_recv.at[j, p, way],
-            device_id=ring(1 if way == 0 else 3), device_id_type=MESH,
+            device_id=ring((1, 3, 2)[way]), device_id_type=MESH,
         )
 
     def q_copy(j, step):
-        which = near(2)[1] if step == 3 else slot
-        return pltpu.make_async_remote_copy(
-            src_ref=qall.at[j, which], dst_ref=qall.at[j, which],
+        return pltpu.make_async_remote_copy(
+            src_ref=qall.at[j, slot], dst_ref=qall.at[j, slot],
             send_sem=q_send.at[j, step - 1], recv_sem=q_recv.at[j, step - 1],
-            device_id=near(2 if step == 2 else 1)[0], device_id_type=MESH,
+            device_id=near(step)[0], device_id_type=MESH,
         )
 
     def gather(j, p):
@@ -230,49 +221,48 @@
             for zz in range(NZ):
                 qall[j, slot, zz * 32 : zz * 32 + 32] = recv_a[j, zz, 80:112]
         if p < 2:
-            for way in range(2):
+            for way in (2, 0, 1):
                 y_copy(j, p, way).start()
         else:
-            for step in (2, 1):
+            for step in (3, 2, 1):
                 q_copy(j, step).start()
 
-    def forward(j, p):
-        if p < 2:
-            for way in range(2):
-                y_copy(j, p, way).wait_recv()
-                f_copy(j, p, way).start()
-        else:
-            q_copy(j, 2).wait_recv()
-            q_copy(j, 3).start()
-
-    def m_copies(j, step):
+    def pieces(j, step):
+        return ((128, 160), (0, 128)) if j == NJ - 1 and step > 1 else ((0, TOK),)
+
+    def m_copy(j, step, piece):
         device, other = near(step)
-        return (
-            pltpu.make_async_remote_copy(
-                src_ref=obuf.at[j, pl.ds(pl.multiple_of(other * TOK, 32), TOK)], dst_ref=mo.at[j, slot],
-                send_sem=m_send.at[j, step - 1], recv_sem=m_recv.at[j, step - 1],
-                device_id=device, device_id_type=MESH,
-            ),
-            pltpu.make_async_remote_copy(
-                src_ref=pst.at[j, other], dst_ref=mst.at[j, slot],
-                send_sem=n_send.at[j, step - 1], recv_sem=n_recv.at[j, step - 1],
-                device_id=device, device_id_type=MESH,
-            ),
-        )
-
-    def m_arrivals(j, step):
+        first, rows = pieces(j, step)[piece]
+        return pltpu.make_async_remote_copy(
+            src_ref=obuf.at[j, pl.ds(pl.multiple_of(other * TOK + first, 32), rows)],
+            dst_ref=mo.at[j, slot, pl.ds(first, rows)],
+            send_sem=m_send.at[j, step - 1, piece], recv_sem=m_recv.at[j, step - 1, piece],
+            device_id=device, device_id_type=MESH,
+        )
+
+    def m_arrival(j, step, piece):
         device, other = near(step)
-        return (
-            pltpu.make_async_remote_copy(
-                src_ref=mo.at[j, slot], dst_ref=mo.at[j, other],
-                send_sem=m_send.at[j, step - 1], recv_sem=m_recv.at[j, step - 1],
-                device_id=device, device_id_type=MESH,
-            ),
-            pltpu.make_async_remote_copy(
-                src_ref=mst.at[j, slot], dst_ref=mst.at[j, other],
-                send_sem=n_send.at[j, step - 1], recv_sem=n_recv.at[j, step - 1],
-                device_id=device, device_id_type=MESH,
-            ),
+        rows = pl.ds(*pieces(j, step)[piece])
+        return pltpu.make_async_remote_copy(
+            src_ref=mo.at[j, slot, rows], dst_ref=mo.at[j, other, rows],
+            send_sem=m_send.at[j, step - 1, piece], recv_sem=m_recv.at[j, step - 1, piece],
+            device_id=device, device_id_type=MESH,
+        )
+
+    def n_copy(j, step):
+        device, other = near(step)
+        return pltpu.make_async_remote_copy(
+            src_ref=pst.at[j, other], dst_ref=mst.at[j, slot],
+            send_sem=n_send.at[j, step - 1], recv_sem=n_recv.at[j, step - 1],
+            device_id=device, device_id_type=MESH,
+        )
+
+    def n_arrival(j, step):
+        device, other = near(step)
+        return pltpu.make_async_remote_copy(
+            src_ref=mst.at[j, slot], dst_ref=mst.at[j, other],
+            send_sem=n_send.at[j, step - 1], recv_sem=n_recv.at[j, step - 1],
+            device_id=device, device_id_type=MESH,
         )
 
     def attend_rows(j, first, count):
@@ -292,25 +282,29 @@
                 pst[j, first + i, 3 + r : 4 + r, wide] = total[:, lanes]
 
     def attend(j):
-        q_copy(j, 1).wait_recv()
-        q_copy(j, 3).wait_recv()
+        for step in range(1, 4):
+            q_copy(j, step).wait_recv()
         for p in range(2):
-            for way in range(2):
-                f_copy(j, p, way).wait_recv()
+            for way in range(3):
+                y_copy(j, p, way).wait_recv()
         for t in range(NY):
             vt[:, t * TOK : (t + 1) * TOK] = kv[j, t, 1].astype(F32).T.astype(BF16)
         pst[j] = jnp.ones((4, 8, HD), F32)
-        if j < NJ - 1:
+        last = j == NJ - 1
+        if last:
+            attend_rows(j, (1 - xl) * 2, 2)
+        else:
             attend_rows(j, 0, 4)
-        else:
-            attend_rows(j, (1 - xl) * 2, 2)
         for step in (3, 2):
-            for copy in m_copies(j, step):
-                copy.start()
-        if j == NJ - 1:
+            n_copy(j, step).start()
+            m_copy(j, step, 0).start()
+        if last:
             attend_rows(j, xl * 2, 2)
-        for copy in m_copies(j, 1):
-            copy.start()
+        n_copy(j, 1).start()
+        m_copy(j, 1, 0).start()
+        if last:
+            for step in (3, 2):
+                m_copy(j, step, 1).start()
         mo[j, slot] = obuf[j, pl.ds(pl.multiple_of(slot * TOK, 32), TOK), :]
         mst[j, slot] = pst[j, slot]
 
@@ -324,10 +318,9 @@
     def c_own(zz):
         return (xh == c) & (zz == z) & (z // 4 == xl)
 
-    def merge(j):
+    def shares(j):
         for step in range(1, 4):
-            for copy in m_arrivals(j, step):
-                copy.wait_recv()
+            n_arrival(j, step).wait_recv()
         tops = [mst[j, i, 0:3, :] for i in range(4)]
         top = jnp.maximum(jnp.maximum(tops[0], tops[1]), jnp.maximum(tops[2], tops[3]))
         parts = [mst[j, i, 3:6, :] * jnp.exp2(tops[i] - top) for i in range(4)]
@@ -336,29 +329,45 @@
         for r in range(3):
             rows = jnp.concatenate([p[r : r + 1] for p in parts] + [jnp.zeros((124, HD), F32)], axis=0)
             wt[r * HD : (r + 1) * HD] = rows.T
-        at = slot if j < NJ - 1 else c
-        share = wt[pl.ds(pl.multiple_of(at * 32, 32), TOK), :]
-        mixed = share[:, 0:1] * mo[j, 0].astype(F32)
+
+    def merge_rows(j, first, rows):
+        at = c if j == NJ - 1 else slot
+        share = wt[pl.ds(pl.multiple_of(at * 32 + first, 32), rows), :]
+        mixed = share[:, 0:1] * mo[j, 0, first : first + rows].astype(F32)
         for i in range(1, 4):
-            mixed += share[:, i : i + 1] * mo[j, i].astype(F32)
+            mixed += share[:, i : i + 1] * mo[j, i, first : first + rows].astype(F32)
         mixed = mixed.astype(BF16)
-        order = pick((128, 32), lambda r: jnp.where(r % 16 < 4, r // 16 * 4 + r % 16, -1))
-        rest = dot(order, mixed[256:288]).astype(BF16)
-        for zz in range(NZ):
-            cbuf[j, zz, 0:32] = mixed[zz * 32 : zz * 32 + 32]
-            cbuf[j, zz, 32:48] = rest[zz * 16 : zz * 16 + 16]
-
-        @pl.loop(0, NZ)
-        def _(i):
-            zz = (z + outward(i)) % NZ
-
-            @pl.when(c_own(zz))
-            def _():
-                pltpu.make_async_copy(cbuf.at[j, z], recv_c.at[j, xl, z % 4], c_recv.at[j, xl, z % 4]).start()
-
-            @pl.when(jnp.logical_not(c_own(zz)))
-            def _():
-                c_copy(j, zz).start()
+        for n in range(min(rows, 256 - first) // MAIN):
+            cbuf[j, first // MAIN + n, 0:32] = mixed[n * MAIN : (n + 1) * MAIN]
+        if first + rows == TOK:
+            order = pick((128, 32), lambda r: jnp.where(r % 16 < 4, r // 16 * 4 + r % 16, -1))
+            rest = dot(order, mixed[256 - first : TOK - first]).astype(BF16)
+            for zz in range(NZ):
+                cbuf[j, zz, 32:48] = rest[zz * 16 : zz * 16 + 16]
+
+    def c_depart(j, zz):
+        @pl.when(c_own(zz))
+        def _():
+            pltpu.make_async_copy(cbuf.at[j, z], recv_c.at[j, xl, z % 4], c_recv.at[j, xl, z % 4]).start()
+
+        @pl.when(jnp.logical_not(c_own(zz)))
+        def _():
+            c_copy(j, zz).start()
+
+    def merge(j):
+        for step in range(1, 4):
+            m_arrival(j, step, 0).wait_recv()
+        shares(j)
+        if j < NJ - 1:
+            merge_rows(j, 0, TOK)
+            pl.loop(0, NZ)(lambda i: c_depart(j, (z + outward(i)) % NZ))
+        else:
+            merge_rows(j, 128, 160)
+            pl.loop(0, 4)(lambda i: c_depart(j, 4 + (z + i) % 4))
+            for step in (3, 2):
+                m_arrival(j, step, 1).wait_recv()
+            merge_rows(j, 0, 128)
+            pl.loop(0, 4)(lambda i: c_depart(j, (z + i) % 4))
 
     sibling = (1 - c, s, xl)
 
@@ -429,23 +438,14 @@
     gather(0, 0)
     gather(0, 1)
     gather(0, 2)
-    forward(0, 0)
-    forward(0, 1)
     gather(1, 0)
-    forward(0, 2)
     gather(1, 1)
     gather(1, 2)
-    forward(1, 0)
     attend(0)
-    forward(1, 1)
     gather(2, 0)
     gather(2, 1)
-    forward(1, 2)
     gather(2, 2)
-    forward(2, 0)
     attend(1)
-    forward(2, 1)
-    forward(2, 2)
     weights(0)
     merge(0)
     attend(2)
@@ -485,12 +485,12 @@
 
         for step in range(1, 4):
             q_copy(j, step).wait_send()
-            for copy in m_copies(j, step):
-                copy.wait_send()
+            n_copy(j, step).wait_send()
+            for piece in range(len(pieces(j, step))):
+                m_copy(j, step, piece).wait_send()
         for p in range(2):
-            for way in range(2):
+            for way in range(3):
                 y_copy(j, p, way).wait_send()
-                f_copy(j, p, way).wait_send()
         s_copy(j).wait_send()
     for n in range(4):
         d_copy(n).wait_send()
@@ -533,9 +533,8 @@
             dma((4,)), dma((NJ, 4)),
             dma((NJ, 3, NZ)), dma((NJ, 3, NZ)),
             dma((NJ, 3)), dma((NJ, 3)),
-            dma((NJ, 2, 2)), dma((NJ, 2, 2)),
-            dma((NJ, 2, 2)), dma((NJ, 2, 2)),
-            dma((NJ, 3)), dma((NJ, 3)),
+            dma((NJ, 2, 3)), dma((NJ, 2, 3)),
+            dma((NJ, 3, 2)), dma((NJ, 3, 2)),
             dma((NJ, 3)), dma((NJ, 3)),
             dma((NJ, NZ)), dma((NJ, 2, 4)),
             dma((NJ,)), dma((NJ,)),

time: 59.7 us -> 58.4 us (0.978)
  Pallas kernels: 58.9 us -> 57.6 us
    pallas_call x1, Pallas kernels: 58.9 us -> 57.6 us  [shards(): pl.pallas_call(kernel, out_shape=pltpu.VMEM((ROWS, 1536), BF16), in_specs...]
where the time goes in v4:
time: 58.4 us; the launch traced here: 58.3 us
  Pallas kernels  57.6 us (99%)
  local copies, waits for them, and re-layouts  0.65 us (1%)
    pallas_call x1, Pallas kernels, shards(): pl.pallas_call(kernel, out_shape=pltpu.VMEM((ROWS, 1536), BF16), in_specs...  57.6 us

profile of v4, /device:TPU:1, one launch (start us, length us, event | category | flops | bytes accessed | tf_op | source)
XLA Modules:
  0.0 58.3 jit_solution(8775334185373822927)
XLA Ops:
  0.0 57.6 %shard_map.55 = bf16[36,1536]{1,0:T(8,128)(2,1)S(1)} custom-call(bf16[1,36,3072]{2,1,0:T(8,128)(2,1)} %q_hbm.1, bf16[1,36,3072]{2,1,0:T(8,128)(2,1)} %k_hbm.1, bf16[1,36,3072]{2,1,0:T(8,128)(2,1)} %v_hbm.1, bf16[1536,3072]{1,0:T(8,128)(2,1)} %w_ref.1, f32[128,2,40,128]{3,2,1,0:T(8,128)} %constant.2.clone.tab_ref), custom_call_target="tpu_custom_call" | custom-call | flops 2400000000 | bytes 8000000 | tf_op jit(solution)/shard_map/pallas_call | solution.py:502
  57.6 0.7 %copy.7 = bf16[36,1536]{1,0:T(8,128)(2,1)} copy(bf16[36,1536]{1,0:T(8,128)(2,1)S(1)} %shard_map.55) | data formatting | bytes 221184

commit v5 on v4

--- a/solution.py
+++ b/solution.py
@@ -104,10 +104,9 @@
 
     @pl.loop(0, NZ)
     def _(zz):
-        for blk in range(2):
-            @pl.when(jnp.logical_not((xh == c) & (zz == z) & (xl == blk)))
-            def _():
-                pl.semaphore_signal(barrier, inc=1, device_id=far(zz, blk), device_id_type=MESH)
+        @pl.when(jnp.logical_not((xh == c) & (zz == z)))
+        def _():
+            pl.semaphore_signal(barrier, inc=1, device_id=far(zz, xl), device_id_type=MESH)
 
     for step in range(1, 4):
         pl.semaphore_signal(barrier, inc=1, device_id=ring(step), device_id_type=MESH)
@@ -423,7 +422,7 @@
             d_copy(3).start()
 
     prepare(0)
-    pl.semaphore_wait(barrier, jnp.where(xh == c, 21, 22))
+    pl.semaphore_wait(barrier, jnp.where(xh == c, 13, 14))
     depart(0, 0)
     depart(0, 1)
     depart(0, 2)

time: 58.4 us -> 58.9 us (level)
  no operation moved by 1% of the time
where the time goes in v5:
time: 58.9 us; the launch traced here: 58.5 us
  Pallas kernels  57.9 us (98%)
  local copies, waits for them, and re-layouts  0.65 us (1%)
    pallas_call x1, Pallas kernels, shards(): pl.pallas_call(kernel, out_shape=pltpu.VMEM((ROWS, 1536), BF16), in_specs...  57.9 us

profile of v5, /device:TPU:1, one launch (start us, length us, event | category | flops | bytes accessed | tf_op | source)
XLA Modules:
  0.0 58.5 jit_solution(15353429505419672297)
XLA Ops:
  0.0 57.9 %shard_map.55 = bf16[36,1536]{1,0:T(8,128)(2,1)S(1)} custom-call(bf16[1,36,3072]{2,1,0:T(8,128)(2,1)} %q_hbm.1, bf16[1,36,3072]{2,1,0:T(8,128)(2,1)} %k_hbm.1, bf16[1,36,3072]{2,1,0:T(8,128)(2,1)} %v_hbm.1, bf16[1536,3072]{1,0:T(8,128)(2,1)} %w_ref.1, f32[128,2,40,128]{3,2,1,0:T(8,128)} %constant.2.clone.tab_ref), custom_call_target="tpu_custom_call" | custom-call | flops 2400000000 | bytes 8000000 | tf_op jit(solution)/shard_map/pallas_call | solution.py:501
  57.9 0.7 %copy.7 = bf16[36,1536]{1,0:T(8,128)(2,1)} copy(bf16[36,1536]{1,0:T(8,128)(2,1)S(1)} %shard_map.55) | data formatting | bytes 221184
